TPU v7x, 32 devices: a whole 2x2x4 slice. The times are simulated.
32 devices in a mesh: grp: 2 (over y), row: 8 (over z, x), head: 2 (over core).
Axes of the slice: x: 2, y: 2, z: 4, core: 2. Of those that a mesh axis runs over, the one named last changes fastest.
Arguments:
- latent: bfloat16 [16, 256, 512], P(('grp', 'row')), parts along dimension 0, may hold values from -6 to 6
- weights: bfloat16 [512, 8, 512], P(None, None, 'head'), may hold values from -0.25 to 0.25
- cotangent: bfloat16 [16, 256, 512], P(('grp', 'row')), parts along dimension 0, may hold values from -6 to 6
Outputs:
- latent_grad: bfloat16 [16, 256, 512], P(('grp', 'row')), parts along dimension 0
- weight_grad: float32 [1024, 8, 512], P(('grp', 'row'), None, 'head'), parts along dimension 0
There are 2 independent parts, one for each index of `grp`. A program takes and returns all parts, laid end to end along the dimension named above; an argument that names none is the same for every part. Nothing has to cross between parts.
All inputs are finite; a program needn't handle non-finite values.
Results may differ from a plain program's by a relative error of at most 0.03.
Values may be sent and summed in bfloat16 or wider, within the bound.
A program may use at most 64 MiB of HBM per device.

v0:
```python
import math
import jax
import jax.numpy as jnp
from jax import lax
from jax.sharding import PartitionSpec as P

HEAD_DIM = 64
epsilon = 1e-06


def index_pair(pattern):
    return (pattern + "hd", pattern.replace("l", "m") + "hd")


def head_norm(values):
    inverse = lax.rsqrt(jnp.mean(values * values, axis=-1, keepdims=True) + epsilon)
    return (values * inverse, inverse)


def three_maps(weights, first):
    width = weights.shape[0]
    return weights[:, first : first + 3, :].reshape(width, 3 * weights.shape[2])


def attend_local(inputs, weights, first, pattern):
    outer, inner, width = inputs.shape
    local = weights.shape[2]
    heads_here = local // HEAD_DIM
    logit_scale = 2.0 / math.sqrt(HEAD_DIM)
    flat = inputs.reshape(outer * inner, width)
    joined = jnp.dot(flat, three_maps(weights, first), preferred_element_type=jnp.float32)
    shaped = joined.reshape(outer, inner, 3, heads_here, HEAD_DIM)
    query_n, query_r = head_norm(shaped[:, :, 0])
    key_n, key_r = head_norm(shaped[:, :, 1])
    query_batched = query_n.astype(jnp.bfloat16)
    key_batched = key_n.astype(jnp.bfloat16)
    value_batched = shaped[:, :, 2].astype(jnp.bfloat16)
    query_ix, key_ix = index_pair(pattern)
    attention_logits = logit_scale * jnp.einsum(
        query_ix + "," + key_ix + "->shlm",
        query_batched,
        key_batched,
        preferred_element_type=jnp.float32,
    )
    expo = jnp.exp(attention_logits)
    probs = expo / jnp.sum(expo, axis=-1, keepdims=True)
    probability_batched = probs.astype(jnp.bfloat16)
    attention_output = jnp.einsum(
        "shlm," + key_ix + "->" + query_ix,
        probability_batched,
        value_batched,
        preferred_element_type=jnp.float32,
    ).astype(jnp.bfloat16)
    saved = (
        query_n,
        query_r,
        query_batched,
        key_n,
        key_r,
        key_batched,
        value_batched,
        probs,
        probability_batched,
    )
    return (flat, saved, attention_output.reshape(outer * inner, local))


def attend_back(saved, upstream, weights, first, pattern):
    outer, inner, width = upstream.shape
    local = weights.shape[2]
    heads_here = local // HEAD_DIM
    logit_scale = 2.0 / math.sqrt(HEAD_DIM)
    (
        query_n,
        query_r,
        query_batched,
        key_n,
        key_r,
        key_batched,
        value_batched,
        probs,
        probability_batched,
    ) = saved
    query_ix, key_ix = index_pair(pattern)
    grad_flat = upstream.reshape(outer * inner, width)
    grad_att = jnp.dot(
        grad_flat, weights[:, first + 3, :], preferred_element_type=jnp.float32
    ).astype(jnp.bfloat16)
    grad_att = grad_att.reshape(outer, inner, heads_here, HEAD_DIM)
    gradient_value_rows = jnp.einsum(
        "shlm," + query_ix + "->" + key_ix,
        probability_batched,
        grad_att,
        preferred_element_type=jnp.float32,
    ).astype(jnp.bfloat16)
    gradient_probability = jnp.einsum(
        query_ix + "," + key_ix + "->shlm",
        grad_att,
        value_batched,
        preferred_element_type=jnp.float32,
    )
    delta = jnp.sum(probs * gradient_probability, axis=-1, keepdims=True)
    gradient_logits = (probs * (gradient_probability - delta)).astype(jnp.bfloat16)
    gradient_normed_query = logit_scale * jnp.einsum(
        "shlm," + key_ix + "->" + query_ix,
        gradient_logits,
        key_batched,
        preferred_element_type=jnp.float32,
    )
    gradient_normed_key = logit_scale * jnp.einsum(
        "shlm," + query_ix + "->" + key_ix,
        gradient_logits,
        query_batched,
        preferred_element_type=jnp.float32,
    )
    grad_query = (
        query_r
        * (
            gradient_normed_query
            - query_n * jnp.mean(gradient_normed_query * query_n, axis=-1, keepdims=True)
        )
    ).astype(jnp.bfloat16)
    grad_key = (
        key_r
        * (
            gradient_normed_key
            - key_n * jnp.mean(gradient_normed_key * key_n, axis=-1, keepdims=True)
        )
    ).astype(jnp.bfloat16)
    stacked = jnp.stack([grad_query, grad_key, gradient_value_rows], axis=2).reshape(
        outer * inner, 3 * local
    )
    partial_in = lax.dot_general(
        stacked,
        three_maps(weights, first),
        (((1,), (1,)), ((), ())),
        preferred_element_type=jnp.float32,
    )
    return (partial_in, stacked, grad_flat)


def weight_terms(flat, stacked, grad_flat, attention_output, count):
    contract = (((0,), (0,)), ((), ()))
    three = lax.dot_general(flat, stacked, contract, preferred_element_type=jnp.float32)
    last = lax.dot_general(
        grad_flat, attention_output, contract, preferred_element_type=jnp.float32
    )
    return jnp.concatenate((three.reshape(count, 3, -1), last.reshape(count, 1, -1)), 1)


def head_sum(partial_value):
    return lax.psum(partial_value.astype(jnp.bfloat16), "head").astype(jnp.float32)


def on_device(latent, weights, cotangent):
    rows, cols, width = latent.shape
    rows_here = width // lax.axis_size("row")
    flat_row, saved_row, attended_row = attend_local(latent, weights, 0, "sl")
    mixed = head_sum(
        lax.dot_general(
            attended_row,
            weights[:, 3, :],
            (((1,), (1,)), ((), ())),
            preferred_element_type=jnp.float32,
        )
    )
    first_out = (latent.astype(jnp.float32) + mixed.reshape(rows, cols, width)).astype(jnp.bfloat16)
    columns, cotangent_cols = (
        lax.all_to_all(first_out, "row", split_axis=1, concat_axis=0, tiled=True),
        lax.all_to_all(cotangent, "row", split_axis=1, concat_axis=0, tiled=True),
    )
    height = columns.shape[0]
    flat_col, saved_col, attended_col = attend_local(columns, weights, 4, "ls")
    partial_col, stacked_col, grad_col = attend_back(saved_col, cotangent_cols, weights, 4, "ls")
    grad_mid = (
        cotangent_cols.astype(jnp.float32) + head_sum(partial_col).reshape(columns.shape)
    ).astype(jnp.bfloat16)
    grad_first = lax.all_to_all(grad_mid, "row", split_axis=0, concat_axis=1, tiled=True)
    partial_row, stacked_row, grad_row = attend_back(saved_row, grad_first, weights, 0, "sl")
    latent_grad = (
        grad_first.astype(jnp.float32) + head_sum(partial_row).reshape(latent.shape)
    ).astype(jnp.bfloat16)
    summed = lax.psum_scatter(
        jnp.concatenate(
            (
                weight_terms(
                    flat_row, stacked_row, grad_row, attended_row, rows_here * lax.axis_size("row")
                ),
                weight_terms(
                    flat_col, stacked_col, grad_col, attended_col, rows_here * lax.axis_size("row")
                ),
            ),
            1,
        ),
        "row",
        scatter_dimension=0,
        tiled=True,
    )
    weight_grad = summed * (1.0 / math.sqrt(height * cols))
    return (latent_grad, weight_grad)


def solution(mesh):
    in_specs = (P(("grp", "row"), None, None), P(None, None, "head"), P(("grp", "row"), None, None))
    out_specs = (P(("grp", "row"), None, None), P(("grp", "row"), None, "head"))
    return jax.shard_map(
        on_device, mesh=mesh, in_specs=in_specs, out_specs=out_specs, check_vma=False
    )
```

profile of v0, /device:TPU:0, one launch (start us, length us, event | category | flops | bytes accessed | tf_op | source)
XLA Modules:
  0.0 247.7 jit_solution(1502684918247256493)
XLA Ops:
  7.2 4.4 %fusion.70 = (bf16[512,1,256]{2,1,0:T(2,128)(2,1)}, bf16[512,1,256]{2,1,0:T(2,128)(2,1)}) fusion(bf16[512,8,256]{2,1,0:T(8,128)(2,1)} %param.4), kind=kLoop, calls=%fused_computation.123 | loop fusion | bytes 1048576 | tf_op jit(solution)/shard_map/slice | solution.py:162
  11.7 0.7 fusion.69
  12.3 0.9 copy.132
  13.3 0.4 convolution_bitcast_fusion
  14.4 0.4 fusion.15
  15.1 0.8 copy-done.15
  15.9 1.0 fusion.2
  16.9 2.1 copy.187
  19.0 0.5 broadcast.179
  19.6 3.0 %reduce.8 = bf16[256,512]{1,0:T(8,128)(2,1)S(1)} reduce(bf16[256,1,512]{2,1,0:T(2,128)(2,1)} %bitcast.232, bf16[]{:T(256)} %broadcast.179), dimensions={1}, to_apply=%bitcast.221.reduce_sub_computation | reduce | bytes 524290
  22.6 0.9 reshape.315
  23.5 7.3 %all-to-all-start = ((bf16[8,2,8192]{2,1,0:T(2,128)(2,1)}), bf16[8,2,8192]{2,1,0:T(2,128)(2,1)}, u32[]{:S(2)}, u32[]{:S(2)}) async-start(bf16[8,2,8192]{2,1,0:T(2,128)(2,1)} %reshape.315), calls=%async_computation | async-start | bytes 524288 | tf_op jit(solution)/shard_map/all_to_all | solution.py:170
  30.7 7.3 %all-reduce.4.cloned.1.call-done = bf16[1,256,512]{2,1,0:T(8,128)(2,1)} async-done(((bf16[1,256,512]{2,1,0:T(8,128)(2,1)}), bf16[1,256,512]{2,1,0:T(8,128)(2,1)}) %all-reduce.4.cloned.1.call-update) | async-done | bytes 262160 | tf_op jit(solution)/shard_map/psum | solution.py:152
  38.0 1.0 add_convert_fusion.1
  39.0 0.4 copy.186
  39.4 2.8 %reduce.9 = bf16[256,512]{1,0:T(8,128)(2,1)} reduce(bf16[256,1,512]{2,1,0:T(2,128)(2,1)S(1)} %bitcast.233, bf16[]{:T(256)} %broadcast.179), dimensions={1}, to_apply=%bitcast.220.reduce_sub_computation | reduce | bytes 524290
  42.3 1.8 reshape.317
  44.1 5.8 %all-to-all-start.1 = ((bf16[8,2,8192]{2,1,0:T(2,128)(2,1)}), bf16[8,2,8192]{2,1,0:T(2,128)(2,1)}, u32[]{:S(2)}, u32[]{:S(2)}) async-start(bf16[8,2,8192]{2,1,0:T(2,128)(2,1)} %reshape.317), calls=%async_computation.1 | async-start | bytes 524288 | tf_op jit(solution)/shard_map/all_to_all | solution.py:169
  50.1 1.6 copy.134
  51.8 1.2 reshape.316
  53.0 0.7 copy-done.6
  53.9 0.9 reshape.296
  54.8 4.5 %all-to-all-done.1 = bf16[8,2,8192]{2,1,0:T(2,128)(2,1)} async-done(((bf16[8,2,8192]{2,1,0:T(2,128)(2,1)}), bf16[8,2,8192]{2,1,0:T(2,128)(2,1)}, u32[]{:S(2)}, u32[]{:S(2)}) %all-to-all-start.1) | async-done | bytes 262176 | tf_op jit(solution)/shard_map/all_to_all | solution.py:169
  59.4 1.2 reshape.318
  60.6 0.7 copy-done.1
  61.4 1.8 fusion.75
  63.1 0.4 multiply_reduce_fusion.3
  63.6 0.6 copy-done.17
  64.2 1.2 fusion.44
  65.8 0.7 copy-done.12
  66.6 1.2 fusion.1
  67.8 3.3 %multiply_reduce_fusion.1 = (f32[32,4,8]{2,1,0:T(4,128)}, f32[32,4,8,8]{2,3,1,0:T(8,128)}) fusion(f32[32,4,8,8]{2,3,1,0:T(8,128)} %fusion.44, bf16[8,32,4,64]{3,1,2,0:T(8,128)(2,1)} %copy-done.12, bf16[8,32,4,64]{3,1,2,0:T(8,128)(2,1)} %copy-done.14), kind=kOutput, calls=%fused_computation.46 | convolution fusion | flops 1081351 | bytes 331776 | tf_op jit(solution)/shard_map/div | solution.py:46
  71.1 1.4 multiply_convert_fusion.1
  72.4 2.0 fusion.49
  74.5 1.1 fusion.41
  75.6 2.4 fusion.46
  78.0 1.1 copy.185
  79.2 2.1 fusion.11
  81.4 1.0 fusion.22
  82.6 1.3 copy.109
  83.9 1.9 reshape.297
  85.9 1.1 convolution_convert_fusion.2
  87.0 17.4 %all-reduce.6.cloned.1.call-done = bf16[8,32,512]{2,1,0:T(8,128)(2,1)} async-done(((bf16[8,32,512]{2,1,0:T(8,128)(2,1)}), bf16[8,32,512]{2,1,0:T(8,128)(2,1)}) %all-reduce.6.cloned.1.call-update) | async-done | bytes 262160 | tf_op jit(solution)/shard_map/psum | solution.py:152
  104.4 1.7 fusion.7
  106.1 5.9 %all-to-all-start.2 = ((bf16[8,32,512]{2,1,0:T(8,128)(2,1)}), bf16[8,32,512]{2,1,0:T(8,128)(2,1)}, u32[]{:S(2)}, u32[]{:S(2)}) async-start(bf16[8,32,512]{2,1,0:T(8,128)(2,1)} %fusion.7), calls=%async_computation.2 | async-start | bytes 524288 | tf_op jit(solution)/shard_map/all_to_all | solution.py:178
  112.0 2.4 fusion.3
  114.4 1.1 copy.113
  115.5 1.1 copy.117
  116.8 0.9 copy.114
  117.7 1.1 convolution_bitcast_fusion.1
  118.8 1.5 fusion.28
  120.3 1.2 all-to-all-done.2
  121.5 1.4 convolution_convert_fusion.5
  123.7 0.7 copy-done.23
  125.2 0.5 copy-done.11
  126.3 1.1 convolution_convert_fusion.1
  127.4 2.0 convolution_bitcast_fusion.2
  129.5 1.7 copy.119
  131.1 4.1 %pad_maximum_fusion = f32[512,8,256]{2,0,1:T(8,128)} fusion(f32[512,1,256]{2,0,1:T(8,128)} %convolution_bitcast_fusion.1, f32[512,3,256]{2,0,1:T(8,128)S(1)} %fusion.28, f32[512,1,256]{2,0,1:T(8,128)} %convolution_bitcast_fusion.2, f32[512,3,256]{2,0,1:T(8,128)} %copy.119), kind=kLoop, calls=%fused_computation | loop fusion | flops 3145728 | bytes 8388608 | tf_op jit(solution)/shard_map/concatenate | solution.py:184
  135.2 10.7 %all-reduce.8.cloned.1.call-done = bf16[256,512]{1,0:T(8,128)(2,1)} async-done(((bf16[256,512]{1,0:T(8,128)(2,1)}), bf16[256,512]{1,0:T(8,128)(2,1)}) %all-reduce.8.cloned.1.call-update) | async-done | bytes 262160 | tf_op jit(solution)/shard_map/psum | solution.py:152
  145.9 1.8 fusion.20
  147.7 91.2 %reduce-scatter.2.cloned.1.call-done = f32[64,8,256]{2,0,1:T(8,128)} async-done(((f32[512,8,256]{2,0,1:T(8,128)}), f32[64,8,256]{2,0,1:T(8,128)}) %reduce-scatter.2.cloned.1.call-update) | async-done | bytes 524304 | tf_op jit(solution)/shard_map/reduce_scatter | solution.py:183
  239.0 1.1 broadcast_multiply_fusion
  240.1 1.1 copy.120
  (87 shorter events, 4.6 us)
Async XLA Ops:
  7.2 30.8 %all-reduce.4.cloned.1.call-start = ((), (), s32[]{:S(2)}) async-start(), calls=%async_computation.4 | async-start | bytes 524288 | tf_op jit(solution)/shard_map/psum | solution.py:152
  7.2 4.4 %copy-start.3 = (bf16[512,8,256]{2,1,0:T(8,128)(2,1)S(1)}, bf16[512,8,256]{2,1,0:T(8,128)(2,1)}, u32[]{:S(2)}) copy-start(bf16[512,8,256]{2,1,0:T(8,128)(2,1)} %param.4) | copy-start | bytes 6291460
  12.3 1.0 copy-start.10
  13.2 0.9 copy-start.8
  13.8 0.6 copy-start.26
  13.8 0.6 copy-start.28
  14.1 0.7 copy-start.20
  14.1 0.7 copy-start.22
  14.8 1.0 copy-start.15
  23.5 20.6 %all-to-all-start = ((bf16[8,2,8192]{2,1,0:T(2,128)(2,1)}), bf16[8,2,8192]{2,1,0:T(2,128)(2,1)}, u32[]{:S(2)}, u32[]{:S(2)}) async-start(bf16[8,2,8192]{2,1,0:T(2,128)(2,1)} %reshape.315), calls=%async_computation | async-start | bytes 524288 | tf_op jit(solution)/shard_map/all_to_all | solution.py:170
  44.1 15.3 %all-to-all-start.1 = ((bf16[8,2,8192]{2,1,0:T(2,128)(2,1)}), bf16[8,2,8192]{2,1,0:T(2,128)(2,1)}, u32[]{:S(2)}, u32[]{:S(2)}) async-start(bf16[8,2,8192]{2,1,0:T(2,128)(2,1)} %reshape.317), calls=%async_computation.1 | async-start | bytes 524288 | tf_op jit(solution)/shard_map/all_to_all | solution.py:169
  49.9 54.5 %all-reduce.6.cloned.1.call-start = ((), (), s32[]{:S(2)}) async-start(), calls=%async_computation.5 | async-start | bytes 524288 | tf_op jit(solution)/shard_map/psum | solution.py:152
  50.1 3.6 %copy-start.16 = (bf16[512,1,256]{2,1,0:T(2,128)(2,1)S(1)}, bf16[512,1,256]{2,1,0:T(2,128)(2,1)}, u32[]{:S(2)}) copy-start(bf16[512,1,256]{2,1,0:T(2,128)(2,1)} %get-tuple-element.21) | copy-start | bytes 786436
  53.0 0.7 copy-start.6
  60.6 0.8 copy-start.1
  61.4 2.9 %copy-start.19 = (bf16[8,32,4,64]{3,2,1,0:T(4,128)(2,1)S(1)}, bf16[8,32,4,64]{3,2,1,0:T(4,128)(2,1)}, u32[]{:S(2)}) copy-start(bf16[8,32,4,64]{3,2,1,0:T(4,128)(2,1)} %reshape.296) | copy-start | bytes 393220
  63.5 0.7 copy-start.17
  64.2 1.2 copy-start.24
  65.8 0.7 copy-start.12
  65.8 0.8 copy-start.14
  71.1 3.4 %copy-start.13 = (bf16[8,32,4,64]{3,1,2,0:T(8,128)(2,1)S(1)}, bf16[8,32,4,64]{3,1,2,0:T(8,128)(2,1)}, u32[]{:S(2)}) copy-start(bf16[8,32,4,64]{3,1,2,0:T(8,128)(2,1)} %copy-done.12) | copy-start | bytes 393220
  78.0 3.3 %copy-start.4 = (f32[32,4,64,8]{2,3,1,0:T(8,128)S(1)}, f32[32,4,64,8]{2,3,1,0:T(8,128)}, u32[]{:S(2)}) copy-start(f32[32,4,64,8]{2,3,1,0:T(8,128)} %fusion.49) | copy-start | bytes 786436
  78.0 3.3 %copy-start.5 = (f32[32,4,64,8]{2,3,1,0:T(8,128)S(1)}, f32[32,4,64,8]{2,3,1,0:T(8,128)}, u32[]{:S(2)}) copy-start(f32[32,4,64,8]{2,3,1,0:T(8,128)} %fusion.41) | copy-start | bytes 786436
  78.0 3.3 %copy-start.25 = (f32[8,32,4]{1,2,0:T(4,128)S(1)}, f32[8,32,4]{1,2,0:T(4,128)}, u32[]{:S(2)}) copy-start(f32[8,32,4]{1,2,0:T(4,128)} %copy-done.24) | copy-start | bytes 12292
  82.6 3.3 %copy-start = (bf16[512,3,256]{0,2,1:T(8,128)(2,1)S(1)}, bf16[512,3,256]{0,2,1:T(8,128)(2,1)}, u32[]{:S(2)}) copy-start(bf16[512,3,256]{0,2,1:T(8,128)(2,1)} %copy.134) | copy-start | bytes 2359300
  83.9 20.5 %copy-start.7 = (bf16[1,256,512]{2,1,0:T(8,128)(2,1)S(1)}, bf16[1,256,512]{2,1,0:T(8,128)(2,1)}, u32[]{:S(2)}) copy-start(bf16[1,256,512]{2,1,0:T(8,128)(2,1)} %copy-done.6) | copy-start | bytes 786436
  86.9 25.1 %copy-start.18 = (bf16[8,32,4,64]{3,1,2,0:T(8,128)(2,1)S(1)}, bf16[8,32,4,64]{3,1,2,0:T(8,128)(2,1)}, u32[]{:S(2)}) copy-start(bf16[8,32,4,64]{3,1,2,0:T(8,128)(2,1)} %copy-done.17) | copy-start | bytes 393220
  106.1 8.3 %copy-start.2 = (bf16[256,1,512]{2,1,0:T(2,128)(2,1)S(1)}, bf16[256,1,512]{2,1,0:T(2,128)(2,1)}, u32[]{:S(2)}) copy-start(bf16[256,1,512]{2,1,0:T(2,128)(2,1)} %copy-done.1) | copy-start | bytes 786436
  106.1 15.4 %all-to-all-start.2 = ((bf16[8,32,512]{2,1,0:T(8,128)(2,1)}), bf16[8,32,512]{2,1,0:T(8,128)(2,1)}, u32[]{:S(2)}, u32[]{:S(2)}) async-start(bf16[8,32,512]{2,1,0:T(8,128)(2,1)} %fusion.7), calls=%async_computation.2 | async-start | bytes 524288 | tf_op jit(solution)/shard_map/all_to_all | solution.py:178
  112.0 34.0 %all-reduce.8.cloned.1.call-start = ((), (), s32[]{:S(2)}) async-start(), calls=%async_computation.6 | async-start | bytes 524288 | tf_op jit(solution)/shard_map/psum | solution.py:152
  123.5 0.9 copy-start.23
  123.5 1.2 copy-start.21
  123.5 1.2 copy-start.27
  123.6 1.2 copy-start.29
  124.7 1.0 copy-start.11
  125.1 1.2 copy-start.9
  127.4 111.6 %reduce-scatter.2.cloned.1.call-start = ((), (), s32[]{:S(2)}) async-start(), calls=%async_computation.7 | async-start | bytes 4718592 | tf_op jit(solution)/shard_map/reduce_scatter | solution.py:183
Sparse Core Ops, SparseCore 0:
  17.0 20.9 all-reduce.3
  87.1 17.2 all-reduce.5
  127.5 18.3 all-reduce.7
  149.9 89.0 reduce-scatter.1
where the time goes:
time: 249 us; the launch traced here: 248 us
  waiting for transfers between devices  132 us (53%)
  local copies, waits for them, and re-layouts  33 us (13%)
  matrix products  27.3 us (11%)
  other arithmetic  21.5 us (9%)
  starting transfers between devices  19.3 us (8%)
  between operations  14.3 us (6%)
    reduce_scatter x1, waiting for transfers between devices, on_device(): lax.psum_scatter(jnp.concatenate((weight_terms(flat_row, stacked_row, gra...  91.2 us
    psum x3, waiting for transfers between devices, head_sum(): lax.psum(partial_value.astype(jnp.bfloat16), 'head').astype(jnp.float32)  35.4 us
    unnamed x70, local copies, waits for them, and re-layouts  17.2 us
    all_to_all x1, starting transfers between devices, on_device(): lax.all_to_all(cotangent, 'row', split_axis=1, concat_axis=0, tiled=True)  7.26 us
    all_to_all x1, starting transfers between devices, on_device(): lax.all_to_all(grad_mid, 'row', split_axis=0, concat_axis=1, tiled=True)  5.9 us
    unnamed x2, other arithmetic  5.87 us
    all_to_all x1, starting transfers between devices, on_device(): lax.all_to_all(first_out, 'row', split_axis=1, concat_axis=0, tiled=True)  5.77 us
  transfers between devices with their start and end apart: 7, of which 6 were waited for; matrix products, arithmetic and copies ran while one was open for 14% of the time, Pallas kernels for 0%

commit v1 on v0

--- a/solution.py
+++ b/solution.py
@@ -6,6 +6,11 @@
 
 HEAD_DIM = 64
 epsilon = 1e-06
+
+
+def gather_and_add(x, axis):
+    parts = lax.all_gather(x, axis)
+    return jnp.sum(parts, axis=0)
 
 
 def index_pair(pattern):
@@ -149,7 +154,7 @@
 
 
 def head_sum(partial_value):
-    return lax.psum(partial_value.astype(jnp.bfloat16), "head").astype(jnp.float32)
+    return gather_and_add(partial_value.astype(jnp.bfloat16), "head").astype(jnp.float32)
 
 
 def on_device(latent, weights, cotangent):

time: 249 us -> 215 us (0.86)
  waiting for transfers between devices: 132 us -> 89 us
  blocking collectives: 0 us -> 6.76 us
  starting transfers between devices: 19.3 us -> 16 us
  local copies, waits for them, and re-layouts: 33 us -> 36.1 us
    psum x3 -> x0, waiting for transfers between devices: 35.4 us -> none  [head_sum(): lax.psum(partial_value.astype(jnp.bfloat16), 'head').astype(jnp.float32)]
    reduce_scatter x1, waiting for transfers between devices: 91.2 us -> 81.5 us  [on_device(): lax.psum_scatter(jnp.concatenate((weight_terms(flat_row, stacked_row, gra...]
    all_gather x0 -> x3, blocking collectives: none -> 6.76 us  [gather_and_add(): parts = lax.all_gather(x, axis)]
    all_to_all x1, waiting for transfers between devices: 0.01 us -> 3.32 us  [on_device(): lax.all_to_all(cotangent, 'row', split_axis=1, concat_axis=0, tiled=True)]
    all_to_all x1, waiting for transfers between devices: 4.54 us -> 1.59 us  [on_device(): lax.all_to_all(first_out, 'row', split_axis=1, concat_axis=0, tiled=True)]
    all_to_all x1, starting transfers between devices: 7.26 us -> 4.41 us  [on_device(): lax.all_to_all(cotangent, 'row', split_axis=1, concat_axis=0, tiled=True)]
    unnamed x70 -> x66, local copies, waits for them, and re-layouts: 17.2 us -> 18.5 us
  transfers between devices with their start and end apart: 7 -> 4, of which waited for: 6 -> 4; matrix products, arithmetic and copies ran while one was open for 14% -> 10% of each run, Pallas kernels for 0% -> 0%
where the time goes in v1:
time: 215 us; the launch traced here: 213 us
  waiting for transfers between devices  89 us (41%)
  local copies, waits for them, and re-layouts  36.1 us (17%)
  matrix products  28.3 us (13%)
  other arithmetic  22.2 us (10%)
  starting transfers between devices  16 us (7%)
  between operations  14.5 us (7%)
  blocking collectives  6.76 us (3%)
    reduce_scatter x1, waiting for transfers between devices, on_device(): lax.psum_scatter(jnp.concatenate((weight_terms(flat_row, stacked_row, gra...  81.5 us
    unnamed x66, local copies, waits for them, and re-layouts  18.5 us
    all_to_all x1, starting transfers between devices, on_device(): lax.all_to_all(first_out, 'row', split_axis=1, concat_axis=0, tiled=True)  7.18 us
    all_gather x3, blocking collectives, gather_and_add(): parts = lax.all_gather(x, axis)  6.76 us
    unnamed x2, other arithmetic  5.78 us
    slice x1, local copies, waits for them, and re-layouts, on_device(): weights[:, 3, :]  4.42 us
    all_to_all x1, starting transfers between devices, on_device(): lax.all_to_all(cotangent, 'row', split_axis=1, concat_axis=0, tiled=True)  4.41 us
  transfers between devices with their start and end apart: 4, of which 4 were waited for; matrix products, arithmetic and copies ran while one was open for 10% of the time, Pallas kernels for 0%

profile of v1, /device:TPU:0, one launch (start us, length us, event | category | flops | bytes accessed | tf_op | source)
XLA Modules:
  0.0 213.0 jit_solution(524430708681247044)
XLA Ops:
  7.2 4.4 %fusion.70 = (bf16[512,1,256]{2,1,0:T(2,128)(2,1)}, bf16[512,1,256]{2,1,0:T(2,128)(2,1)}) fusion(bf16[512,8,256]{2,1,0:T(8,128)(2,1)} %param.4), kind=kLoop, calls=%fused_computation.123 | loop fusion | bytes 1048576 | tf_op jit(solution)/shard_map/slice | solution.py:167
  11.6 0.7 fusion.69
  12.3 0.9 copy.134
  15.0 0.8 copy-done.15
  16.1 2.4 %all-gather = bf16[512,512]{1,0:T(8,128)(2,1)} all-gather(bf16[256,512]{1,0:T(8,128)(2,1)S(1)} %convolution_convert_fusion.3), channel_id=2, replica_groups=mesh['grp'=2,'row'=8,'head'=2] {'head'}, dimensions={0}, use_global_device_ids=true | all-gather | bytes 786432 | tf_op jit(solution)/shard_map/all_gather | solution.py:12
  18.5 1.1 reduce_sum.147
  20.1 0.6 broadcast.179
  20.7 2.9 %reduce.12 = bf16[256,512]{1,0:T(8,128)(2,1)} reduce(bf16[256,1,512]{2,1,0:T(2,128)(2,1)S(1)} %bitcast.241, bf16[]{:T(256)} %broadcast.179), dimensions={1}, to_apply=%bitcast.228.reduce_sub_computation | reduce | bytes 524290
  23.6 1.9 reshape.350
  25.5 7.2 %all-to-all-start.1 = ((bf16[8,2,8192]{2,1,0:T(2,128)(2,1)}), bf16[8,2,8192]{2,1,0:T(2,128)(2,1)}, u32[]{:S(2)}, u32[]{:S(2)}) async-start(bf16[8,2,8192]{2,1,0:T(2,128)(2,1)} %reshape.350), calls=%async_computation.1 | async-start | bytes 524288 | tf_op jit(solution)/shard_map/all_to_all | solution.py:174
  32.6 1.4 copy.189
  34.0 2.9 %reduce.11 = bf16[256,512]{1,0:T(8,128)(2,1)} reduce(bf16[256,1,512]{2,1,0:T(2,128)(2,1)S(1)} %bitcast.244, bf16[]{:T(256)} %broadcast.179), dimensions={1}, to_apply=%bitcast.229.reduce_sub_computation | reduce | bytes 524290
  36.9 1.9 reshape.348
  38.8 1.6 copy.136
  40.4 1.6 all-to-all-done.1
  42.0 4.4 %all-to-all-start = ((bf16[8,2,8192]{2,1,0:T(2,128)(2,1)}), bf16[8,2,8192]{2,1,0:T(2,128)(2,1)}, u32[]{:S(2)}, u32[]{:S(2)}) async-start(bf16[8,2,8192]{2,1,0:T(2,128)(2,1)} %reshape.348), calls=%async_computation | async-start | bytes 524288 | tf_op jit(solution)/shard_map/all_to_all | solution.py:175
  46.4 1.2 reshape.351
  47.6 0.8 copy-done.1
  48.4 1.7 fusion.75
  50.1 1.0 multiply_reduce_fusion.3
  51.1 0.8 fusion.24
  51.8 3.3 %all-to-all-done = bf16[8,2,8192]{2,1,0:T(2,128)(2,1)} async-done(((bf16[8,2,8192]{2,1,0:T(2,128)(2,1)}), bf16[8,2,8192]{2,1,0:T(2,128)(2,1)}, u32[]{:S(2)}, u32[]{:S(2)}) %all-to-all-start) | async-done | bytes 262176 | tf_op jit(solution)/shard_map/all_to_all | solution.py:175
  55.1 1.9 reshape.349
  57.0 1.1 copy.92
  58.1 0.7 copy-done.6
  58.8 1.9 convolution_convert_fusion.6
  60.7 1.8 reshape.325
  62.5 0.7 add_rsqrt_fusion.1
  63.2 0.7 add_rsqrt_fusion
  64.0 2.2 %fusion.44 = f32[32,4,8,8]{2,3,1,0:T(8,128)} fusion(bf16[8,32,4,64]{3,1,2,0:T(8,128)(2,1)} %fusion.24, bf16[8,32,4,64]{3,2,1,0:T(4,128)(2,1)} %reshape.325), kind=kOutput, calls=%fused_computation.95 | convolution fusion | flops 1048576 | bytes 294912 | tf_op jit(solution)/shard_map/lshd,mshd->shlm/dot_general | solution.py:101
  66.6 0.7 copy-done.12
  67.4 1.2 fusion.1
  68.6 3.3 %multiply_reduce_fusion.1 = (f32[32,4,8]{2,1,0:T(4,128)}, f32[32,4,8,8]{2,3,1,0:T(8,128)}) fusion(f32[32,4,8,8]{2,3,1,0:T(8,128)} %fusion.44, bf16[8,32,4,64]{3,1,2,0:T(8,128)(2,1)} %copy-done.12, bf16[8,32,4,64]{3,1,2,0:T(8,128)(2,1)} %copy-done.14), kind=kOutput, calls=%fused_computation.48 | convolution fusion | flops 1081351 | bytes 331776 | tf_op jit(solution)/shard_map/div | solution.py:51
  71.8 1.4 multiply_convert_fusion.1
  73.2 2.0 fusion.49
  75.2 1.2 fusion.41
  76.4 2.4 %fusion.46 = bf16[32,4,64,8]{2,3,1,0:T(8,128)(2,1)} fusion(bf16[8,32,4,64]{3,2,1,0:T(4,128)(2,1)} %reshape.325, f32[32,4,8,8]{2,3,1,0:T(8,128)} %fusion.1), kind=kOutput, calls=%fused_computation.97 | convolution fusion | flops 1065991 | bytes 294912 | tf_op jit(solution)/shard_map/shlm,lshd->mshd/dot_general | solution.py:95
  78.8 1.1 copy.187
  79.9 2.1 %fusion.12 = (f32[8,32,4]{1,2,0:T(4,128)S(1)}, f32[8,32,4]{1,2,0:T(4,128)S(1)}) fusion(f32[32,4,64,8]{2,3,1,0:T(8,128)} %fusion.41, f32[8,32,3,4,64]{4,1,3,2,0:T(8,128)S(1)} %fusion.75, f32[8,32,4]{1,2,0:T(4,128)S(1)} %add_rsqrt_fusion.1, f32[8,32,4]{1,2,0:T(4,128)} %copy-done.22, f32[32,4,64,8]{2,3,1,0:T(8,128)} %fusion.49), kind=kLoop, calls=%fused_computation.41 | loop fusion | flops 522240 | bytes 1064960 | tf_op jit(solution)/shard_map/reduce_sum | solution.py:125
  82.1 1.0 fusion.22
  83.4 1.3 copy.111
  84.7 1.9 reshape.326
  87.0 2.2 %all-gather.1 = bf16[512,512]{1,0:T(8,128)(2,1)S(1)} all-gather(bf16[256,512]{1,0:T(8,128)(2,1)S(1)} %convolution_convert_fusion.2), channel_id=3, replica_groups=mesh['grp'=2,'row'=8,'head'=2] {'head'}, dimensions={0}, use_global_device_ids=true | all-gather | bytes 786432 | tf_op jit(solution)/shard_map/all_gather | solution.py:12
  89.3 0.8 fusion.7
  90.0 4.2 %all-to-all-start.2 = ((bf16[8,32,512]{2,1,0:T(8,128)(2,1)}), bf16[8,32,512]{2,1,0:T(8,128)(2,1)}, u32[]{:S(2)}, u32[]{:S(2)}) async-start(bf16[8,32,512]{2,1,0:T(8,128)(2,1)} %fusion.7), calls=%async_computation.2 | async-start | bytes 524288 | tf_op jit(solution)/shard_map/all_to_all | solution.py:183
  94.5 1.7 fusion.2
  96.2 1.1 copy.115
  97.6 0.9 copy.116
  98.6 1.1 convolution_bitcast_fusion.1
  99.6 1.5 fusion.28
  101.1 2.6 %all-to-all-done.2 = bf16[8,32,512]{2,1,0:T(8,128)(2,1)} async-done(((bf16[8,32,512]{2,1,0:T(8,128)(2,1)}), bf16[8,32,512]{2,1,0:T(8,128)(2,1)}, u32[]{:S(2)}, u32[]{:S(2)}) %all-to-all-start.2) | async-done | bytes 262176 | tf_op jit(solution)/shard_map/all_to_all | solution.py:183
  103.7 1.4 convolution_convert_fusion.5
  105.1 2.0 convolution_bitcast_fusion.2
  108.0 0.7 copy-done.21
  109.4 0.5 copy-done.11
  110.0 1.5 fusion.34
  111.5 1.9 copy.121
  113.4 3.5 %pad_maximum_fusion = f32[512,8,256]{2,0,1:T(8,128)} fusion(f32[512,1,256]{2,0,1:T(8,128)} %convolution_bitcast_fusion.1, f32[512,3,256]{2,0,1:T(8,128)S(1)} %fusion.28, f32[512,1,256]{2,0,1:T(8,128)} %convolution_bitcast_fusion.2, f32[512,3,256]{2,0,1:T(8,128)S(1)} %copy.121), kind=kLoop, calls=%fused_computation | loop fusion | flops 3145728 | bytes 8388608 | tf_op jit(solution)/shard_map/concatenate | solution.py:189
  116.9 1.1 copy-done.9
  118.5 2.2 %all-gather.2 = bf16[512,512]{1,0:T(8,128)(2,1)S(1)} all-gather(bf16[256,512]{1,0:T(8,128)(2,1)S(1)} %convolution_convert_fusion.1), channel_id=4, replica_groups=mesh['grp'=2,'row'=8,'head'=2] {'head'}, dimensions={0}, use_global_device_ids=true | all-gather | bytes 786432 | tf_op jit(solution)/shard_map/all_gather | solution.py:12
  120.8 1.7 fusion.6
  122.5 81.5 %reduce-scatter.2.cloned.1.call-done = f32[64,8,256]{2,0,1:T(8,128)} async-done(((f32[512,8,256]{2,0,1:T(8,128)}), f32[64,8,256]{2,0,1:T(8,128)}) %reduce-scatter.2.cloned.1.call-update) | async-done | bytes 524304 | tf_op jit(solution)/shard_map/reduce_scatter | solution.py:188
  204.0 1.1 broadcast_multiply_fusion
  205.1 1.1 copy.122
  (80 shorter events, 6.3 us)
Async XLA Ops:
  7.2 4.4 %copy-start.3 = (bf16[512,8,256]{2,1,0:T(8,128)(2,1)S(1)}, bf16[512,8,256]{2,1,0:T(8,128)(2,1)}, u32[]{:S(2)}) copy-start(bf16[512,8,256]{2,1,0:T(8,128)(2,1)} %param.4) | copy-start | bytes 6291460
  12.3 1.0 copy-start.10
  13.2 0.9 copy-start.8
  13.7 0.6 copy-start.24
  13.7 0.6 copy-start.26
  14.1 0.7 copy-start.18
  14.1 0.7 copy-start.20
  14.8 1.0 copy-start.15
  25.5 16.5 %all-to-all-start.1 = ((bf16[8,2,8192]{2,1,0:T(2,128)(2,1)}), bf16[8,2,8192]{2,1,0:T(2,128)(2,1)}, u32[]{:S(2)}, u32[]{:S(2)}) async-start(bf16[8,2,8192]{2,1,0:T(2,128)(2,1)} %reshape.350), calls=%async_computation.1 | async-start | bytes 524288 | tf_op jit(solution)/shard_map/all_to_all | solution.py:174
  42.0 13.2 %all-to-all-start = ((bf16[8,2,8192]{2,1,0:T(2,128)(2,1)}), bf16[8,2,8192]{2,1,0:T(2,128)(2,1)}, u32[]{:S(2)}, u32[]{:S(2)}) async-start(bf16[8,2,8192]{2,1,0:T(2,128)(2,1)} %reshape.348), calls=%async_computation | async-start | bytes 524288 | tf_op jit(solution)/shard_map/all_to_all | solution.py:175
  47.6 0.8 copy-start.1
  58.1 0.7 copy-start.6
  64.0 2.2 %copy-start.22 = (f32[8,32,4]{1,2,0:T(4,128)}, f32[8,32,4]{1,2,0:T(4,128)S(1)}, u32[]{:S(2)}) copy-start(f32[8,32,4]{1,2,0:T(4,128)S(1)} %add_rsqrt_fusion) | copy-start | bytes 12292
  66.6 0.7 copy-start.12
  66.6 0.8 copy-start.14
  71.8 3.4 %copy-start.13 = (bf16[8,32,4,64]{3,1,2,0:T(8,128)(2,1)S(1)}, bf16[8,32,4,64]{3,1,2,0:T(8,128)(2,1)}, u32[]{:S(2)}) copy-start(bf16[8,32,4,64]{3,1,2,0:T(8,128)(2,1)} %copy-done.12) | copy-start | bytes 393220
  78.8 3.3 %copy-start.4 = (f32[32,4,64,8]{2,3,1,0:T(8,128)S(1)}, f32[32,4,64,8]{2,3,1,0:T(8,128)}, u32[]{:S(2)}) copy-start(f32[32,4,64,8]{2,3,1,0:T(8,128)} %fusion.49) | copy-start | bytes 786436
  78.8 3.3 %copy-start.5 = (f32[32,4,64,8]{2,3,1,0:T(8,128)S(1)}, f32[32,4,64,8]{2,3,1,0:T(8,128)}, u32[]{:S(2)}) copy-start(f32[32,4,64,8]{2,3,1,0:T(8,128)} %fusion.41) | copy-start | bytes 786436
  78.8 3.3 %copy-start.23 = (f32[8,32,4]{1,2,0:T(4,128)S(1)}, f32[8,32,4]{1,2,0:T(4,128)}, u32[]{:S(2)}) copy-start(f32[8,32,4]{1,2,0:T(4,128)} %copy-done.22) | copy-start | bytes 12292
  83.4 3.2 %copy-start = (bf16[512,3,256]{0,2,1:T(8,128)(2,1)S(1)}, bf16[512,3,256]{0,2,1:T(8,128)(2,1)}, u32[]{:S(2)}) copy-start(bf16[512,3,256]{0,2,1:T(8,128)(2,1)} %copy.136) | copy-start | bytes 2359300
  86.6 2.7 %copy-start.7 = (bf16[1,256,512]{2,1,0:T(8,128)(2,1)S(1)}, bf16[1,256,512]{2,1,0:T(8,128)(2,1)}, u32[]{:S(2)}) copy-start(bf16[1,256,512]{2,1,0:T(8,128)(2,1)} %copy-done.6) | copy-start | bytes 786436
  90.0 6.2 %copy-start.2 = (bf16[256,1,512]{2,1,0:T(2,128)(2,1)S(1)}, bf16[256,1,512]{2,1,0:T(2,128)(2,1)}, u32[]{:S(2)}) copy-start(bf16[256,1,512]{2,1,0:T(2,128)(2,1)} %copy-done.1) | copy-start | bytes 786436
  90.0 13.7 %all-to-all-start.2 = ((bf16[8,32,512]{2,1,0:T(8,128)(2,1)}), bf16[8,32,512]{2,1,0:T(8,128)(2,1)}, u32[]{:S(2)}, u32[]{:S(2)}) async-start(bf16[8,32,512]{2,1,0:T(8,128)(2,1)} %fusion.7), calls=%async_computation.2 | async-start | bytes 524288 | tf_op jit(solution)/shard_map/all_to_all | solution.py:183
  94.2 109.8 %reduce-scatter.2.cloned.1.call-start = ((), (), s32[]{:S(2)}) async-start(), calls=%async_computation.4 | async-start | bytes 4718592 | tf_op jit(solution)/shard_map/reduce_scatter | solution.py:188
  107.8 0.9 copy-start.21
  107.8 1.2 copy-start.19
  107.8 1.2 copy-start.25
  107.8 1.2 copy-start.27
  109.0 1.0 copy-start.11
  109.4 2.0 copy-start.16
  116.9 1.1 copy-start.9
  116.9 1.2 copy-start.17
Sparse Core Ops, SparseCore 0:
  117.1 86.8 reduce-scatter.1
